TPU v7x, 32 devices: a whole 2x2x4 slice. The times are simulated.
32 devices in a mesh: sub: 8 (over z, x), col: 4 (over y, core).
Axes of the slice: x: 2, y: 2, z: 4, core: 2. Of those that a mesh axis runs over, the one named last changes fastest.
Arguments:
- control: float32 [768, 1536, 32], P('sub', 'col'), may hold values from -6 to 6
- scale_index: int32 [32], replicated, may hold values from 0 to 7
- length_x: float32 [8, 3], replicated, may hold values from 3 to 150
- length_y: float32 [8, 3], replicated, may hold values from 3 to 80
- scale_weight: float32 [8, 3], replicated, may hold values from 0.3 to 1
Outputs:
- increment: float32 [768, 1536, 32], P('sub', 'col')
- wind: bfloat16 [2, 768, 1536, 32], P(None, 'sub', 'col')
All inputs are finite; a program needn't handle non-finite values.
Results may differ from a plain program's by a relative error of at most 0.001.
Values sent between devices are 32-bit elements; how exact they have to be, the bound alone decides.
A program may use at most 128 MiB of HBM per device.

v0:
```python
import jax
import jax.numpy as jnp
from jax import lax
from jax.sharding import PartitionSpec as P

wind_gain = 2.0
highest = lax.Precision.HIGHEST


def with_halo(array, sides, width):
    for axis, dim in sides:
        size, length = (lax.axis_size(axis), array.shape[dim])
        up = [(i, (i + 1) % size) for i in range(size - 1)]
        down = [(j, i) for i, j in up]
        last = lax.slice_in_dim(array, length - width, length, axis=dim)
        initial = lax.slice_in_dim(array, 0, width, axis=dim)
        before = lax.ppermute(last, axis, up)
        after = lax.ppermute(initial, axis, down)
        array = jnp.concatenate([before, array, after], axis=dim)
    return array


def lift_powers(inv_len, extent, reverse):
    offsets = jnp.arange(extent, dtype=jnp.float32)
    if reverse:
        return jnp.exp(-(extent - offsets)[None] * inv_len[:, None])
    return jnp.exp(-(offsets + 1.0)[None] * inv_len[:, None])


def decay_table(inv_len, extent, reverse, weighted):
    offsets = jnp.arange(extent, dtype=jnp.float32)
    spacing = offsets[:, None] - offsets[None, :]
    if reverse:
        spacing = -spacing
    falloff = jnp.exp(-jnp.maximum(spacing, 0.0)[None] * inv_len[:, None, None])
    if weighted:
        falloff = falloff * (1.0 - jnp.exp(-inv_len))[:, None, None]
    return jnp.where((spacing >= 0.0)[None], falloff, 0.0)


def place(matrix, rank, first_pos, second_pos):
    shape = [1] * rank
    shape[first_pos] = matrix.shape[0]
    shape[second_pos] = matrix.shape[1]
    return matrix.reshape(shape)


def local_solve(source, inv_len, along, reverse, slab_axis):
    shape = source.shape
    extent = shape[along]
    tile_len = 128
    tiles = extent // tile_len
    kernel = decay_table(inv_len, tile_len, reverse, True)
    lifting = lift_powers(inv_len, tile_len, reverse)
    chained = decay_table(inv_len * tile_len, tiles, reverse, False)
    edge_at = 0 if reverse else tile_len - 1
    letters = ["p", "q", "r"]
    letters[slab_axis] = "s"

    def spec(tile_letter, inner):
        return "".join((tile_letter + inner if k == along else letters[k] for k in range(3)))

    pieces = source.reshape(shape[:along] + (tiles, tile_len) + shape[along + 1 :])
    within = jnp.einsum(
        spec("t", "j") + ",sij->" + spec("t", "i"), pieces, kernel, precision=highest
    )
    edge = lax.index_in_dim(within, edge_at, along + 1, keepdims=False)
    carried = jnp.einsum(spec("t", "") + ",sct->" + spec("c", ""), edge, chained, precision=highest)
    zero_pad = jnp.zeros_like(lax.slice_in_dim(carried, 0, 1, axis=along))
    if reverse:
        incoming = jnp.concatenate(
            [lax.slice_in_dim(carried, 1, tiles, axis=along), zero_pad], axis=along
        )
        outgoing = lax.index_in_dim(carried, 0, along, keepdims=False)
    else:
        incoming = jnp.concatenate(
            [zero_pad, lax.slice_in_dim(carried, 0, tiles - 1, axis=along)], axis=along
        )
        outgoing = lax.index_in_dim(carried, tiles - 1, along, keepdims=False)
    result = within + place(lifting, 4, slab_axis, along + 1) * jnp.expand_dims(incoming, along + 1)
    return (result.reshape(shape), outgoing)


def plain_pass(source, inv_len, along, reverse, slab_axis):
    return local_solve(source, inv_len, along, reverse, slab_axis)[0]


def multiscale(source, inv_x, inv_y, amplitude, sweep, slab_axis, x_axis, y_axis):
    total = jnp.zeros_like(source)
    shape = [1, 1, 1]
    shape[slab_axis] = source.shape[slab_axis]
    for scale in range(inv_x.shape[1]):
        smoothed = sweep(source, inv_x[:, scale], x_axis, False, slab_axis)
        smoothed = sweep(smoothed, inv_x[:, scale], x_axis, True, slab_axis)
        smoothed = sweep(smoothed, inv_y[:, scale], y_axis, False, slab_axis)
        smoothed = sweep(smoothed, inv_y[:, scale], y_axis, True, slab_axis)
        total = total + amplitude[:, scale].reshape(shape) * smoothed
    return total


def slab_coefficients(scale_index, length_x, length_y, scale_weight):
    kinds = length_x.shape[0]
    picks = (scale_index[:, None] == jnp.arange(kinds, dtype=jnp.int32)[None]).astype(jnp.float32)
    along_x = jnp.sum(picks[:, :, None] * length_x[None], axis=1)
    along_y = jnp.sum(picks[:, :, None] * length_y[None], axis=1)
    chosen = jnp.sum(picks[:, :, None] * scale_weight[None], axis=1)
    return (1.0 / along_x, 1.0 / along_y, 4.0 * chosen * jnp.sqrt(along_x * along_y))


def halo_wind(increment):
    padded = with_halo(increment, (("sub", 0), ("col", 1)), 1)
    north = padded[2:, 1:-1] - padded[:-2, 1:-1]
    east = padded[1:-1, 2:] - padded[1:-1, :-2]
    return jnp.stack([-wind_gain * north, wind_gain * east]).astype(jnp.bfloat16)


def send_back(stacked, sub_count, col_count, band_rows, band_cols):
    layers = stacked.shape[0]
    arranged = stacked.reshape(layers, sub_count, band_rows, col_count, band_cols).transpose(
        1, 3, 0, 2, 4
    )
    arranged = arranged.reshape(sub_count, col_count * layers, band_rows * band_cols)
    returned = lax.all_to_all(
        arranged.reshape(sub_count * col_count * layers, band_rows * band_cols),
        ("sub", "col"),
        split_axis=0,
        concat_axis=0,
        tiled=True,
    )
    return returned.reshape(sub_count * col_count, layers, band_rows, band_cols)


def per_device(control, scale_index, length_x, length_y, scale_weight):
    inv_x, inv_y, amplitude = slab_coefficients(scale_index, length_x, length_y, scale_weight)
    sub_count = lax.axis_size("sub")
    col_count = lax.axis_size("col")
    band_rows, band_cols, total_slabs = control.shape
    per_dev = total_slabs // (sub_count * col_count)
    first_slab = (lax.axis_index("sub") * col_count + lax.axis_index("col")) * per_dev
    mine_x = lax.dynamic_slice_in_dim(inv_x, first_slab, per_dev, 0)
    mine_y = lax.dynamic_slice_in_dim(inv_y, first_slab, per_dev, 0)
    mine_amp = lax.dynamic_slice_in_dim(amplitude, first_slab, per_dev, 0)
    flat = control.transpose(2, 0, 1).reshape(total_slabs, band_rows * band_cols)
    arrived = lax.all_to_all(flat, ("sub", "col"), split_axis=0, concat_axis=0, tiled=True)
    slabs_here = arrived.reshape(sub_count, col_count, per_dev, band_rows, band_cols).transpose(
        2, 0, 3, 1, 4
    )
    slabs_here = slabs_here.reshape(per_dev, sub_count * band_rows, col_count * band_cols)
    filtered = multiscale(slabs_here, mine_x, mine_y, mine_amp, plain_pass, 0, 2, 1)
    returned = send_back(filtered, sub_count, col_count, band_rows, band_cols)
    increment = returned.reshape(total_slabs, band_rows, band_cols).transpose(1, 2, 0)
    return (increment, halo_wind(increment))


def solution(mesh):
    placed = (P("sub", "col", None), P(), P(), P(), P())
    return jax.shard_map(
        per_device,
        mesh=mesh,
        in_specs=placed,
        out_specs=(P("sub", "col", None), P(None, "sub", "col", None)),
        check_vma=False,
    )
```

profile of v0, /device:TPU:0, one launch (start us, length us, event | category | flops | bytes accessed | tf_op | source)
XLA Modules:
  0.0 475.7 jit_solution(15784411777190576737)
XLA Ops:
  0.6 7.3 %copy.56 = f32[32,96,384]{2,1,0:T(8,128)} copy(f32[32,96,384]{2,0,1:T(8,128)} %bitcast.311) | data formatting | bytes 9437184 | tf_op jit(solution)/shard_map/transpose | solution.py:143
  7.9 7.7 %all_to_all.16 = f32[32,1,36864]{2,1,0:T(1,128)} reshape(f32[32,96,384]{2,1,0:T(8,128)} %copy.56) | data formatting | bytes 9437184 | tf_op jit(solution)/shard_map/all_to_all | solution.py:144
  15.6 7.6 %all-to-all-start = ((f32[32,1,36864]{2,1,0:T(1,128)}), f32[32,1,36864]{2,1,0:T(1,128)}, u32[]{:S(2)}, u32[]{:S(2)}) async-start(f32[32,1,36864]{2,1,0:T(1,128)} %all_to_all.16), calls=%async_computation | async-start | bytes 9437184 | tf_op jit(solution)/shard_map/all_to_all | solution.py:144
  23.5 0.6 fusion.283
  25.3 0.5 fusion.282
  32.2 0.6 multiply_exponential_fusion.3
  32.9 0.6 multiply_exponential_fusion.2
  33.5 0.6 multiply_exponential_fusion.7
  34.2 0.6 multiply_exponential_fusion.6
  34.8 0.6 multiply_exponential_fusion.11
  35.5 0.6 multiply_exponential_fusion.10
  36.1 0.6 multiply_exponential_fusion.1
  36.7 0.6 multiply_exponential_fusion
  37.4 0.6 multiply_exponential_fusion.5
  38.0 0.6 multiply_exponential_fusion.4
  38.6 0.6 multiply_exponential_fusion.9
  39.2 0.6 multiply_exponential_fusion.8
  40.1 0.6 fusion.281
  40.7 88.3 %all-to-all-done = f32[32,1,36864]{2,1,0:T(1,128)} async-done(((f32[32,1,36864]{2,1,0:T(1,128)}), f32[32,1,36864]{2,1,0:T(1,128)}, u32[]{:S(2)}, u32[]{:S(2)}) %all-to-all-start) | async-done | bytes 4718624 | tf_op jit(solution)/shard_map/all_to_all | solution.py:144
  128.9 15.2 %reduce = f32[32,36864]{1,0:T(8,128)} reduce(f32[32,1,36864]{2,1,0:T(1,128)} %all-to-all-done, f32[]{:T(128)} %constant.73), dimensions={1}, to_apply=%all_to_all.13.reduce_sub_computation | reduce | bytes 9437188 | tf_op jit(solution)/shard_map/all_to_all | solution.py:144
  144.1 5.4 %copy.103 = f32[4,8,96,384]{3,2,1,0:T(8,128)} copy(f32[4,8,96,384]{3,1,2,0:T(8,128)} %bitcast.308) | data formatting | bytes 9437184
  149.5 6.2 %copy.58 = f32[8,4,1,96,384]{3,0,4,1,2:T(8,128)} copy(f32[8,4,1,96,384]{4,3,1,0,2:T(8,128)} %bitcast.310) | data formatting | bytes 9437184 | tf_op jit(solution)/shard_map/reshape | solution.py:145
  155.7 7.4 %reshape.1527 = f32[768,12,128]{0,2,1:T(8,128)} reshape(f32[1,8,96,4,384]{2,1,4,3,0:T(8,128)} %bitcast.298) | data formatting | bytes 9437184 | tf_op jit(solution)/shard_map/reshape.7
  163.1 7.3 %fusion.62 = f32[128,768,12]{1,0,2:T(8,128)S(1)} fusion(f32[768,12,128]{0,2,1:T(8,128)} %reshape.1527, f32[]{:T(128)} %bitcast.78, f32[]{:T(128)} %bitcast.77), kind=kOutput, calls=%fused_computation.82 | convolution fusion | flops 1812054016 | bytes 9437192 | tf_op jit(solution)/shard_map/sqtj,sij->sqti/dot_general | solution.py:64
  170.6 5.8 %fusion.10 = f32[768,12,128]{0,2,1:T(8,128)S(1)} fusion(f32[128,768,12]{1,0,2:T(8,128)S(1)} %fusion.62, f32[768,12]{0,1:T(8,128)S(1)} %pad_bitcast_fusion.3, f32[128]{0:T(128)S(1)} %multiply_exponential_fusion.3, f32[]{:T(128)} %bitcast.78, f32[]{:T(128)} %bitcast.77), kind=kOutput, calls=%fused_computation.20 | convolution fusion | flops 1814429696 | bytes 9474568 | tf_op jit(solution)/shard_map/sqtj,sij->sqti/dot_general | solution.py:64
  176.7 2.7 multiply_add_fusion.1
  179.4 6.8 %reshape.1560 = f32[6,128,1536]{1,0,2:T(8,128)} reshape(f32[768,12,128]{0,2,1:T(8,128)} %multiply_add_fusion.1) | data formatting | bytes 9437184 | tf_op jit(solution)/shard_map/reshape.151
  186.2 8.5 %fusion.45 = f32[1,6,128,1536]{3,2,1,0:T(8,128)S(1)} fusion(f32[6,128,1536]{1,0,2:T(8,128)} %reshape.1560, f32[]{:T(128)} %bitcast.72, f32[]{:T(128)} %bitcast.71), kind=kOutput, calls=%fused_computation.52 | convolution fusion | flops 1812054016 | bytes 9437192 | tf_op jit(solution)/shard_map/stjr,sij->stir/dot_general | solution.py:64
  195.0 1.9 copy-done.1
  196.9 7.7 %fusion.66 = f32[128,768,12]{1,0,2:T(8,128)S(1)} fusion(f32[768,12,128]{0,2,1:T(8,128)} %reshape.1527, f32[]{:T(128)} %bitcast.44, f32[]{:T(128)} %bitcast.43), kind=kOutput, calls=%fused_computation.86 | convolution fusion | flops 1812054016 | bytes 9437192 | tf_op jit(solution)/shard_map/sqtj,sij->sqti/dot_general | solution.py:64
  204.8 5.8 %fusion.15 = f32[768,12,128]{0,2,1:T(8,128)S(1)} fusion(f32[128,768,12]{1,0,2:T(8,128)S(1)} %fusion.66, f32[768,12]{0,1:T(8,128)S(1)} %pad_bitcast_fusion.7, f32[128]{0:T(128)S(1)} %multiply_exponential_fusion.7, f32[]{:T(128)} %bitcast.44, f32[]{:T(128)} %bitcast.43), kind=kOutput, calls=%fused_computation.26 | convolution fusion | flops 1814429696 | bytes 9474568 | tf_op jit(solution)/shard_map/sqtj,sij->sqti/dot_general | solution.py:64
  210.9 2.8 multiply_add_fusion.2
  213.7 6.6 %reshape.1559 = f32[6,128,1536]{1,0,2:T(8,128)} reshape(f32[768,12,128]{0,2,1:T(8,128)} %multiply_add_fusion.2) | data formatting | bytes 9437184 | tf_op jit(solution)/shard_map/reshape.101
  220.3 8.5 %fusion.42 = f32[1,6,128,1536]{3,2,1,0:T(8,128)S(1)} fusion(f32[6,128,1536]{1,0,2:T(8,128)} %reshape.1559, f32[]{:T(128)} %bitcast.38, f32[]{:T(128)} %bitcast.37), kind=kOutput, calls=%fused_computation.51 | convolution fusion | flops 1812054016 | bytes 9437192 | tf_op jit(solution)/shard_map/stjr,sij->stir/dot_general | solution.py:64
  229.1 2.0 copy-done.2
  231.1 7.4 %fusion.70 = f32[128,768,12]{1,0,2:T(8,128)S(1)} fusion(f32[768,12,128]{0,2,1:T(8,128)} %reshape.1527, f32[]{:T(128)} %bitcast.8, f32[]{:T(128)} %bitcast.7), kind=kOutput, calls=%fused_computation.90 | convolution fusion | flops 1812054016 | bytes 9437192 | tf_op jit(solution)/shard_map/sqtj,sij->sqti/dot_general | solution.py:64
  238.7 5.8 %fusion.20 = f32[768,12,128]{0,2,1:T(8,128)S(1)} fusion(f32[128,768,12]{1,0,2:T(8,128)S(1)} %fusion.70, f32[768,12]{0,1:T(8,128)S(1)} %pad_bitcast_fusion.11, f32[128]{0:T(128)S(1)} %multiply_exponential_fusion.11, f32[]{:T(128)} %bitcast.8, f32[]{:T(128)} %bitcast.7), kind=kOutput, calls=%fused_computation.32 | convolution fusion | flops 1814429696 | bytes 9474568 | tf_op jit(solution)/shard_map/sqtj,sij->sqti/dot_general | solution.py:64
  244.8 2.7 multiply_add_fusion.3
  247.6 6.8 %reshape.1558 = f32[6,128,1536]{1,0,2:T(8,128)} reshape(f32[768,12,128]{0,2,1:T(8,128)} %multiply_add_fusion.3) | data formatting | bytes 9437184 | tf_op jit(solution)/shard_map/reshape.51
  254.4 8.7 %fusion.39 = f32[1,6,128,1536]{3,2,1,0:T(8,128)S(1)} fusion(f32[6,128,1536]{1,0,2:T(8,128)} %reshape.1558, f32[]{:T(128)} %bitcast.2, f32[]{:T(128)} %bitcast.1), kind=kOutput, calls=%fused_computation.50 | convolution fusion | flops 1812054016 | bytes 9437192 | tf_op jit(solution)/shard_map/stjr,sij->stir/dot_general | solution.py:64
  263.4 7.1 %fusion.36 = f32[1,6,128,1536]{3,2,1,0:T(8,128)S(1)} fusion(f32[1,6,128,1536]{3,2,1,0:T(8,128)} %copy-done.1, f32[6,1536]{1,0:T(8,128)S(1)} %pad_bitcast_fusion.1, f32[128]{0:T(128)S(1)} %multiply_exponential_fusion.1, f32[]{:T(128)} %bitcast.72, f32[]{:T(128)} %bitcast.71), kind=kOutput, calls=%fused_computation.49 | convolution fusion | flops 1814429696 | bytes 9474568 | tf_op jit(solution)/shard_map/stjr,sij->stir/dot_general | solution.py:64
  270.7 5.1 %fusion.33 = f32[1,6,128,1536]{3,2,1,0:T(8,128)S(1)} fusion(f32[1,6,128,1536]{3,2,1,0:T(8,128)S(1)} %bitcast.306, f32[6,1536]{1,0:T(8,128)S(1)} %pad_bitcast_fusion.5, f32[128]{0:T(128)S(1)} %multiply_exponential_fusion.5, f32[]{:T(128)} %bitcast.38, f32[]{:T(128)} %bitcast.37), kind=kOutput, calls=%fused_computation.48 | convolution fusion | flops 1814429696 | bytes 9474568 | tf_op jit(solution)/shard_map/stjr,sij->stir/dot_general | solution.py:64
  276.1 5.1 %fusion.30 = f32[1,6,128,1536]{3,2,1,0:T(8,128)S(1)} fusion(f32[1,6,128,1536]{3,2,1,0:T(8,128)S(1)} %fusion.39, f32[6,1536]{1,0:T(8,128)S(1)} %pad_bitcast_fusion.9, f32[128]{0:T(128)S(1)} %multiply_exponential_fusion.9, f32[]{:T(128)} %bitcast.2, f32[]{:T(128)} %bitcast.1), kind=kOutput, calls=%fused_computation.47 | convolution fusion | flops 1814429696 | bytes 9474568 | tf_op jit(solution)/shard_map/stjr,sij->stir/dot_general | solution.py:64
  281.5 5.6 %multiply_add_fusion = f32[1,6,128,1536]{3,2,1,0:T(8,128)} fusion(f32[1,6,128,1536]{3,2,1,0:T(8,128)S(1)} %fusion.36, f32[1,6,128,1536]{3,2,1,0:T(8,128)S(1)} %fusion.33, f32[1,6,128,1536]{3,2,1,0:T(8,128)S(1)} %fusion.30, f32[6,1536]{1,0:T(8,128)S(1)} %pad_bitcast_fusion, f32[128]{0:T(128)S(1)} %multiply_exponential_fusion, f32[]{:T(128)} %bitcast.70, ...), kind=kLoop, calls=%fused_computation.34 | loop fusion | flops 12976128 | bytes 18986508 | tf_op jit(solution)/shard_map/add | solution.py:97
  287.0 6.2 %add.163 = f32[1,8,96,4,384]{4,3,2,1,0:T(4,128)} reshape(f32[1,6,128,1536]{3,2,1,0:T(8,128)} %multiply_add_fusion) | data formatting | bytes 9437184 | tf_op jit(solution)/shard_map/add | solution.py:97
  293.2 5.1 %copy.190 = f32[1,8,96,4,384]{4,2,3,1,0:T(8,128)} copy(f32[1,8,96,4,384]{4,3,2,1,0:T(4,128)} %add.163) | data formatting | bytes 9437184 | tf_op jit(solution)/shard_map/add | solution.py:97
  298.3 8.2 %all_to_all.17 = f32[32,1,36864]{2,1,0:T(1,128)} reshape(f32[8,4,1,96,384]{4,3,1,0,2:T(8,128)} %bitcast.309) | data formatting | bytes 9437184 | tf_op jit(solution)/shard_map/all_to_all | solution.py:123
  306.4 110.7 %all_to_all.20 = f32[32,1,36864]{2,1,0:T(1,128)} all-to-all(f32[32,1,36864]{2,1,0:T(1,128)} %all_to_all.17), channel_id=1, replica_groups=mesh['sub'=8,'col'=4] {'sub','col'}, dimensions={0} | all-to-all | bytes 9437184 | tf_op jit(solution)/shard_map/all_to_all | solution.py:123
  417.1 15.2 %reduce.1 = f32[32,36864]{1,0:T(8,128)} reduce(f32[32,1,36864]{2,1,0:T(1,128)} %all_to_all.20, f32[]{:T(128)} %constant.73), dimensions={1}, to_apply=%all_to_all.15.reduce_sub_computation | reduce | bytes 9437188 | tf_op jit(solution)/shard_map/all_to_all | solution.py:123
  432.3 3.2 copy.104
  435.6 3.2 collective-permute-start.1
  438.8 1.3 collective-permute-start
  440.6 4.3 collective-permute-done
  444.8 0.7 pad_maximum_fusion.11
  445.5 0.6 copy.72
  446.1 1.3 collective-permute-start.3
  447.4 0.6 copy.70
  447.9 1.3 collective-permute-start.2
  449.2 7.3 %copy.74 = f32[96,384,32]{1,2,0:T(8,128)} copy(f32[96,384,32]{1,0,2:T(8,128)} %bitcast.296) | data formatting | bytes 9437184
  456.5 0.6 copy.73
  457.1 0.7 copy.71
  457.8 13.1 %fusion.48 = (bf16[1,96,384,32]{2,1,3,0:T(8,128)(2,1)S(1)}, bf16[1,96,384,32]{2,1,3,0:T(8,128)(2,1)S(1)}) fusion(f32[96,384,32]{1,0,2:T(8,128)} %bitcast.297, f32[1,384,32]{1,0,2:T(1,128)S(1)} %collective-permute-done.1, f32[1,384,32]{1,0,2:T(1,128)S(1)} %collective-permute-done, f32[98,1,32]{1,0,2:T(8,128)S(1)} %copy.73, f32[98,1,32]{1,0,2:T(8,128)S(1)} %copy.71), kind=kLoop, calls=%fused_computation.53 | loop fusion | flops 16515072 | bytes 9560576 | tf_op jit(solution)/shard_map/stack | solution.py:114
  470.9 0.5 pad_maximum_fusion.8
  471.5 4.0 copy.75
  (74 shorter events, 3.7 us)
Async XLA Ops:
  15.6 7.6 %copy-start.6 = (s32[32]{0:T(128)S(1)}, s32[32]{0:T(128)}, u32[]{:S(2)}) copy-start(s32[32]{0:T(128)} %param.6) | copy-start | bytes 388
  15.6 7.6 %copy-start.3 = (f32[8,3]{0,1:T(4,128)S(1)}, f32[8,3]{0,1:T(4,128)}, u32[]{:S(2)}) copy-start(f32[8,3]{0,1:T(4,128)} %param.9) | copy-start | bytes 292
  15.6 7.6 %copy-start.4 = (f32[8,3]{0,1:T(4,128)S(1)}, f32[8,3]{0,1:T(4,128)}, u32[]{:S(2)}) copy-start(f32[8,3]{0,1:T(4,128)} %param.7) | copy-start | bytes 292
  15.6 7.7 %copy-start.5 = (f32[8,3]{0,1:T(4,128)S(1)}, f32[8,3]{0,1:T(4,128)}, u32[]{:S(2)}) copy-start(f32[8,3]{0,1:T(4,128)} %param.8) | copy-start | bytes 292
  15.6 113.3 %all-to-all-start = ((f32[32,1,36864]{2,1,0:T(1,128)}), f32[32,1,36864]{2,1,0:T(1,128)}, u32[]{:S(2)}, u32[]{:S(2)}) async-start(f32[32,1,36864]{2,1,0:T(1,128)} %all_to_all.16), calls=%async_computation | async-start | bytes 9437184 | tf_op jit(solution)/shard_map/all_to_all | solution.py:144
  194.7 2.2 copy-start.1
  228.8 2.2 copy-start.2
  254.3 16.4 %slice-start = ((s8[4718592]{0:T(1024)(128)(4,1)}), s8[4194304]{0:T(1024)(128)(4,1)S(1)}, s32[]{:S(2)}) async-start(s8[4718592]{0:T(1024)(128)(4,1)} %bitcast.305), calls=%async_computation.2 | async-start | bytes 8388608
  263.3 7.4 %slice-start.1 = ((s8[4718592]{0:T(1024)(128)(4,1)}), s8[524288]{0:T(1024)(128)(4,1)S(1)}, s32[]{:S(2)}) async-start(s8[4718592]{0:T(1024)(128)(4,1)} %bitcast.305), calls=%async_computation.3 | async-start | bytes 1048576
  435.5 9.3 %copy-start = (f32[4,8,96,384]{3,2,1,0:T(8,128)}, f32[4,8,96,384]{3,2,1,0:T(8,128)S(1)}, u32[]{:S(2)}) copy-start(f32[4,8,96,384]{3,2,1,0:T(8,128)S(1)} %copy.104) | copy-start | bytes 14155780
  435.6 5.0 %collective-permute-start.1 = (f32[1,384,32]{1,0,2:T(1,128)S(1)}, f32[1,384,32]{1,0,2:T(1,128)S(1)}, u32[]{:S(2)}, u32[]{:S(2)}) collective-permute-start(f32[1,384,32]{1,0,2:T(1,128)S(1)} %get-tuple-element.15), channel_id=1, source_target_pairs={{0,4},{4,8},{8,12},{12,16},{16,20},{20,24},{24,28},{1,5},{5,9},{9,... | collective-permute-start | bytes 147464 | tf_op jit(solution)/shard_map/ppermute | solution.py:17
  438.8 6.0 %collective-permute-start = (f32[1,384,32]{1,0,2:T(1,128)S(1)}, f32[1,384,32]{1,0,2:T(1,128)S(1)}, u32[]{:S(2)}, u32[]{:S(2)}) collective-permute-start(f32[1,384,32]{1,0,2:T(1,128)S(1)} %get-tuple-element.16), channel_id=1, source_target_pairs={{4,0},{8,4},{12,8},{16,12},{20,16},{24,20},{28,24},{5,1},{9,5},{13... | collective-permute-start | bytes 147464 | tf_op jit(solution)/shard_map/ppermute | solution.py:18
  446.1 10.4 %collective-permute-start.3 = (f32[98,1,32]{0,2,1:T(8,128)S(1)}, f32[98,1,32]{0,2,1:T(8,128)S(1)}, u32[]{:S(2)}, u32[]{:S(2)}) collective-permute-start(f32[98,1,32]{0,2,1:T(8,128)S(1)} %copy.72), channel_id=1, source_target_pairs={{0,1},{1,2},{2,3},{4,5},{5,6},{6,7},{8,9},{9,10},{10,11},{12,13},{... | collective-permute-start | bytes 37640 | tf_op jit(solution)/shard_map/ppermute | solution.py:17
  447.9 9.2 %collective-permute-start.2 = (f32[98,1,32]{0,2,1:T(8,128)S(1)}, f32[98,1,32]{0,2,1:T(8,128)S(1)}, u32[]{:S(2)}, u32[]{:S(2)}) collective-permute-start(f32[98,1,32]{0,2,1:T(8,128)S(1)} %copy.70), channel_id=1, source_target_pairs={{1,0},{2,1},{3,2},{5,4},{6,5},{7,6},{9,8},{10,9},{11,10},{13,12},{... | collective-permute-start | bytes 37640 | tf_op jit(solution)/shard_map/ppermute | solution.py:18
where the time goes:
time: 484 us; the launch traced here: 476 us
  blocking collectives  111 us (23%)
  local copies, waits for them, and re-layouts  96.8 us (20%)
  waiting for transfers between devices  93 us (19%)
  matrix products  85.1 us (18%)
  other arithmetic  66.3 us (14%)
  starting transfers between devices  14.7 us (3%)
  between operations  9.15 us (2%)
    all_to_all x1, blocking collectives, send_back(): lax.all_to_all(arranged.reshape(sub_count * col_count * layers, band_rows...  111 us
    all_to_all x1, waiting for transfers between devices, per_device(): lax.all_to_all(flat, ('sub', 'col'), split_axis=0, concat_axis=0, tiled=T...  88.3 us
    dot_general x12, matrix products, local_solve(): jnp.einsum(spec('t', 'j') + ',sij->' + spec('t', 'i'), pieces, kernel, pr...  82.8 us
    another operation x4, local copies, waits for them, and re-layouts  27.5 us
    unnamed x22, local copies, waits for them, and re-layouts  23.8 us
    all_to_all x1, other arithmetic, per_device(): lax.all_to_all(flat, ('sub', 'col'), split_axis=0, concat_axis=0, tiled=T...  15.2 us
    all_to_all x1, other arithmetic, send_back(): lax.all_to_all(arranged.reshape(sub_count * col_count * layers, band_rows...  15.2 us
    another operation x2, other arithmetic, halo_wind(): jnp.stack([-wind_gain * north, wind_gain * east]).astype(jnp.bfloat16)  13.7 us
  transfers between devices with their start and end apart: 5, of which 3 were waited for; matrix products, arithmetic and copies ran while one was open for 4% of the time, Pallas kernels for 0%

commit v1 on v0

v1 whole, which is shorter than its diff:
```python
import functools
import jax
import jax.numpy as jnp
from jax import lax
from jax.experimental import pallas as pl
from jax.experimental.pallas import tpu as pltpu
from jax.sharding import PartitionSpec as P

highest = lax.Precision.HIGHEST
group = 8
vmem_bytes = 56 * 1024 * 1024


def slab_coefficients(scale_index, length_x, length_y, scale_weight):
    kinds = length_x.shape[0]
    picks = (scale_index[:, None] == jnp.arange(kinds, dtype=jnp.int32)[None]).astype(jnp.float32)
    along_x = jnp.sum(picks[:, :, None] * length_x[None], axis=1)
    along_y = jnp.sum(picks[:, :, None] * length_y[None], axis=1)
    chosen = jnp.sum(picks[:, :, None] * scale_weight[None], axis=1)
    return (1.0 / along_x, 1.0 / along_y, 4.0 * chosen * jnp.sqrt(along_x * along_y))


def fwd_weight(is_fwd, src, dst, tile, inv):
    gap = jnp.maximum(dst - 1 - src, 0).astype(jnp.float32) * tile
    return jnp.where(is_fwd & (src < dst), jnp.exp(-gap * inv), 0.0)


def bwd_weight(is_fwd, src, dst, tile, tiles, inv):
    gap = jnp.maximum(src - dst - 1, 0).astype(jnp.float32) * tile
    fold = (1 + tile * (tiles - 1 - dst) + tile * (tiles - 1 - src)).astype(jnp.float32)
    return jnp.where(
        is_fwd, -jnp.exp(-fold * inv), jnp.where(src > dst, jnp.exp(-gap * inv), 0.0)
    )


def edge_weights(inv_x, tile):
    scales = inv_x.shape[1]
    j = jnp.arange(tile, dtype=jnp.float32)
    inv = inv_x[:, :, None]
    gain = 1.0 - jnp.exp(-inv)
    fwd = gain * jnp.exp(-(tile - 1.0 - j) * inv)
    bwd = gain * jnp.exp(-j * inv)
    pad = jnp.zeros((inv_x.shape[0], 8 - 2 * scales, tile), jnp.float32)
    return jnp.concatenate([fwd, bwd, pad], axis=1)


def carry_matrix(inv_x, tile, local, devices, me):
    scales = inv_x.shape[1]
    tiles = local * devices
    q = jnp.arange(tiles * 8, dtype=jnp.int32)[None, :, None]
    k = jnp.arange((local + 1) * 8, dtype=jnp.int32)[None, None, :]
    q_kind, q_tile = q % 8, q // 8
    k_kind, k_tile = k % 8, k // 8
    q_fwd = q_kind < scales
    k_fwd = k_kind < scales
    q_scale = q_kind - jnp.where(q_fwd, 0, scales)
    k_scale = k_kind - jnp.where(k_fwd, 0, scales)
    valid = (q_kind < 2 * scales) & (k_kind < 2 * scales) & (q_scale == k_scale)
    inv = inv_x[:, 0][:, None, None]
    for m in range(1, scales):
        inv = jnp.where(k_scale == m, inv_x[:, m][:, None, None], inv)
    r = jnp.exp(-inv)
    r_tile = jnp.exp(-inv * tile)
    first, last = me * local, me * local + local - 1
    inner = k_tile < local
    dst = jnp.where(inner, first + k_tile, jnp.where(k_fwd, first, last))
    c = fwd_weight(q_fwd, q_tile, dst, tile, inv)
    d = bwd_weight(q_fwd, q_tile, dst, tile, tiles, inv)
    own = q_tile == dst
    left = (c + r * (jnp.where(own & ~q_fwd, 1.0, 0.0) + r_tile * d)) / (1.0 + r)
    right = (r * (jnp.where(own & q_fwd, 1.0, 0.0) + r_tile * c) + d) / (1.0 + r)
    left = jnp.where(me == 0, 0.0, left)
    right = jnp.where(me == devices - 1, 0.0, right)
    value = jnp.where(inner, jnp.where(k_fwd, c, d), jnp.where(k_fwd, left, right))
    return jnp.where(valid, value, 0.0)


def split(value):
    high = value.astype(jnp.bfloat16)
    return high, (value - high.astype(jnp.float32)).astype(jnp.bfloat16)


def edge_kernel(tile, ctrl_ref, weight_ref, out_ref):
    rows, slabs, cols = ctrl_ref.shape
    for s in range(slabs):
        for t in range(cols // tile):
            piece = ctrl_ref[:, s, t * tile : (t + 1) * tile]
            out_ref[s, t * 8 : (t + 1) * 8, :] = lax.dot_general(
                weight_ref[s], piece, (((1,), (1,)), ((), ())),
                precision=highest, preferred_element_type=jnp.float32,
            )


def x_edges(ctrl, weights, tile):
    rows, slabs, cols = ctrl.shape
    local = cols // tile
    return pl.pallas_call(
        functools.partial(edge_kernel, tile),
        grid=(slabs // group,),
        in_specs=[
            pl.BlockSpec((rows, group, cols), lambda i: (0, i, 0)),
            pl.BlockSpec((group, 8, tile), lambda i: (i, 0, 0)),
        ],
        out_specs=pl.BlockSpec((group, local * 8, rows), lambda i: (i, 0, 0)),
        out_shape=jax.ShapeDtypeStruct((slabs, local * 8, rows), jnp.float32),
        compiler_params=pltpu.CompilerParams(vmem_limit_bytes=vmem_bytes),
        name="x_edges",
    )(ctrl, weights)


def x_kernel(tile, scales, ctrl_ref, gath_ref, carry_ref, inv_ref, ry_ref, w_ref, ye_ref):
    rows, slabs, cols = ctrl_ref.shape
    local = cols // tile
    width = w_ref.shape[3]
    lanes = scales * tile
    lane = lax.broadcasted_iota(jnp.int32, (tile, lanes), 1)
    row = lax.broadcasted_iota(jnp.int32, (tile, lanes), 0)
    scale_at = sum((lane >= m * tile).astype(jnp.int32) for m in range(1, scales))
    dist = jnp.abs(row - (lane - scale_at * tile)).astype(jnp.float32)
    one = lax.broadcasted_iota(jnp.int32, (1, lanes), 1)
    one_scale = sum((one >= m * tile).astype(jnp.int32) for m in range(1, scales))
    pos = (one - one_scale * tile).astype(jnp.float32)
    spot = lax.broadcasted_iota(jnp.int32, (rows, width - cols), 1)
    for s in range(slabs):
        inv = inv_ref[s]
        r = jnp.exp(-inv)
        high_k, low_k = split(jnp.exp(-dist * inv) * ((1.0 - r) / (1.0 + r)))
        from_left = jnp.exp(-(pos + 1.0) * inv) / (1.0 + r)
        from_right = jnp.exp(-(tile - pos) * inv) / (1.0 + r)
        gathered = jnp.concatenate([gath_ref[d, s] for d in range(gath_ref.shape[0])], axis=0)
        carry = lax.dot_general(
            gathered, carry_ref[s], (((0,), (0,)), ((), ())),
            precision=highest, preferred_element_type=jnp.float32,
        )
        for t in range(local):
            high, low = split(ctrl_ref[:, s, t * tile : (t + 1) * tile])
            dot = functools.partial(jnp.dot, preferred_element_type=jnp.float32)
            out = dot(high, high_k) + (dot(high, low_k) + dot(low, high_k))
            for m in range(scales):
                part = slice(m * tile, (m + 1) * tile)
                at = t * 8 + m
                w_ref[m, :, s, t * tile : (t + 1) * tile] = (
                    out[:, part]
                    + carry[:, at : at + 1] * from_left[:, part]
                    + carry[:, at + scales : at + scales + 1] * from_right[:, part]
                )
        for m in range(scales):
            at = local * 8 + m
            left = carry[:, at : at + 1]
            right = carry[:, at + scales : at + scales + 1]
            w_ref[m, :, s, cols:] = jnp.where(
                spot == 0, right, jnp.where(spot == width - cols - 1, left, 0.0)
            )

    owners = ye_ref.shape[0]
    each = slabs // owners
    zero = jnp.zeros((slabs, width), jnp.float32)
    rates = [ry_ref[m] for m in range(scales)]

    def widen(value):
        return jnp.concatenate([value] * (width // 128), axis=1)

    def step(y, state):
        fwd, bwd, power = state
        here = [w_ref[m, y] for m in range(scales)]
        fwd = tuple(widen(rates[m]) * fwd[m] + here[m] for m in range(scales))
        bwd = tuple(bwd[m] + widen(power[m]) * here[m] for m in range(scales))
        power = tuple(power[m] * rates[m] for m in range(scales))
        return fwd, bwd, power

    ones = jnp.ones((slabs, 128), jnp.float32)
    fwd, bwd, _ = lax.fori_loop(
        0, rows, step, ((zero,) * scales, (zero,) * scales, (ones,) * scales), unroll=4
    )
    for m in range(scales):
        for o in range(owners):
            mine = slice(o * each, (o + 1) * each)
            ye_ref[o, m * each : (m + 1) * each, :] = fwd[m][mine]
            ye_ref[o, (scales + m) * each : (scales + m + 1) * each, :] = bwd[m][mine]


def x_pass(ctrl, gathered, carry, inv_rows, rate_y, tile, width, subs):
    rows, slabs, cols = ctrl.shape
    scales = rate_y.shape[0]
    cols_n, _, edge_rows, _ = gathered.shape
    each = slabs // subs
    owners = group // each
    lanes = inv_rows.shape[2]
    return pl.pallas_call(
        functools.partial(x_kernel, tile, scales),
        grid=(slabs // group,),
        in_specs=[
            pl.BlockSpec((rows, group, cols), lambda i: (0, i, 0)),
            pl.BlockSpec((cols_n, group, edge_rows, rows), lambda i: (0, i, 0, 0)),
            pl.BlockSpec((group,) + carry.shape[1:], lambda i: (i, 0, 0)),
            pl.BlockSpec((group, 1, lanes), lambda i: (i, 0, 0)),
            pl.BlockSpec((scales, group, 128), lambda i: (0, i, 0)),
        ],
        out_specs=[
            pl.BlockSpec((scales, rows, group, width), lambda i: (0, 0, i, 0)),
            pl.BlockSpec((owners, 2 * scales * each, width), lambda i: (i, 0, 0)),
        ],
        out_shape=[
            jax.ShapeDtypeStruct((scales, rows, slabs, width), jnp.float32),
            jax.ShapeDtypeStruct((subs, 2 * scales * each, width), jnp.float32),
        ],
        compiler_params=pltpu.CompilerParams(vmem_limit_bytes=vmem_bytes),
        name="x_pass",
    )(ctrl, gathered, carry, inv_rows, rate_y)


def y_carries(arrived, inv_y, rows, subs, first_slab, each):
    scales = inv_y.shape[1]
    width = arrived.shape[2]
    inv = lax.dynamic_slice_in_dim(inv_y, first_slab, each, 0).T.reshape(scales * each)
    src = jnp.arange(subs, dtype=jnp.int32)[None, :, None]
    dst = jnp.arange(subs, dtype=jnp.int32)[:, None, None]
    inv = inv[None, None, :]
    r = jnp.exp(-inv)
    r_tile = jnp.exp(-inv * rows)
    parts = []
    for is_fwd in (True, False):
        flag = jnp.full((1, 1, 1), is_fwd)
        c = fwd_weight(flag, src, dst, rows, inv)
        d = bwd_weight(flag, src, dst, rows, subs, inv)
        own = jnp.where((src == dst) & flag, 1.0, 0.0)
        right = (r * (own + r_tile * c) + d) / ((1.0 + r) * (1.0 - r))
        right = jnp.where(dst == subs - 1, 0.0, right)
        parts.append(jnp.concatenate([c, right], axis=2))
    half = scales * each
    total = 0.0
    for a in range(subs):
        fwd = jnp.concatenate([arrived[a, :half]] * 2, axis=0)
        bwd = jnp.concatenate([arrived[a, half:]] * 2, axis=0)
        total = total + parts[0][:, a, :, None] * fwd[None] + parts[1][:, a, :, None] * bwd[None]
    return total


def y_kernel(scales, first_ref, w_ref, carry_ref, par_ref, inc_ref, wind_ref, held):
    _, rows, slabs, width = w_ref.shape
    cols = inc_ref.shape[2]

    def widen(value):
        return jnp.concatenate([value] * (width // 128), axis=1)

    rates = [par_ref[m] for m in range(scales)]
    gains = [par_ref[scales + m] for m in range(scales)]
    start = tuple(carry_ref[m] for m in range(scales))

    def ahead(y, state):
        state = tuple(widen(rates[m]) * state[m] + w_ref[m, y] for m in range(scales))
        for m in range(scales):
            held[m, y] = state[m]
        return state

    lax.fori_loop(0, rows, ahead, start, unroll=2)
    ends = tuple(carry_ref[scales + m] for m in range(scales))

    def mix(state):
        return sum(widen(gains[m]) * state[m] for m in range(scales))

    def back(i, carried):
        y = rows - 1 - i
        state, after, later = carried
        state = tuple(widen(rates[m]) * state[m] + held[m, y] for m in range(scales))
        total = mix(state)
        here = total[:, :cols]
        inc_ref[y] = here
        east = pltpu.roll(total, width - 1, 1)[:, :cols] - pltpu.roll(total, 1, 1)[:, :cols]
        wind_ref[1, y] = (2.0 * east).astype(jnp.bfloat16)

        @pl.when(i > 0)
        def _():
            wind_ref[0, y + 1] = (-2.0 * (later - here)).astype(jnp.bfloat16)

        return state, here, after

    below = mix(ends)[:, :cols]
    state, after, later = lax.fori_loop(0, rows, back, (ends, below, below), unroll=2)
    above = mix(tuple(widen(rates[m]) * state[m] + start[m] for m in range(scales)))[:, :cols]
    above = jnp.where(first_ref[0] == 1, 0.0, above)
    wind_ref[0, 0] = (-2.0 * (later - above)).astype(jnp.bfloat16)


def y_pass(first, smoothed, carries, params, cols):
    scales, rows, slabs, width = smoothed.shape
    block = 16
    return pl.pallas_call(
        functools.partial(y_kernel, scales),
        grid=(slabs // block,),
        in_specs=[
            pl.BlockSpec(memory_space=pltpu.SMEM),
            pl.BlockSpec((scales, rows, block, width), lambda i: (0, 0, i, 0)),
            pl.BlockSpec((2 * scales, block, width), lambda i: (0, i, 0)),
            pl.BlockSpec((2 * scales, block, 128), lambda i: (0, i, 0)),
        ],
        out_specs=[
            pl.BlockSpec((rows, block, cols), lambda i: (0, i, 0)),
            pl.BlockSpec((2, rows, block, cols), lambda i: (0, 0, i, 0)),
        ],
        out_shape=[
            jax.ShapeDtypeStruct((rows, slabs, cols), jnp.float32),
            jax.ShapeDtypeStruct((2, rows, slabs, cols), jnp.bfloat16),
        ],
        scratch_shapes=[pltpu.VMEM((scales, rows, block, width), jnp.float32)],
        compiler_params=pltpu.CompilerParams(vmem_limit_bytes=vmem_bytes),
        name="y_pass",
    )(first, smoothed, carries, params)


def per_device(control, scale_index, length_x, length_y, scale_weight):
    inv_x, inv_y, amplitude = slab_coefficients(scale_index, length_x, length_y, scale_weight)
    subs, cols_n = lax.axis_size("sub"), lax.axis_size("col")
    rows, cols, slabs = control.shape
    scales = inv_x.shape[1]
    tile = 128 if cols % 128 == 0 else cols
    local = cols // tile
    width = (cols // 128 + 1) * 128
    each = slabs // subs
    me = lax.axis_index("sub")
    ctrl = control.transpose(0, 2, 1)
    edges = x_edges(ctrl, edge_weights(inv_x, tile), tile)
    gathered = lax.all_gather(edges, "col")
    carry = carry_matrix(inv_x, tile, local, cols_n, lax.axis_index("col"))
    inv_rows = jnp.repeat(inv_x, tile, axis=1)[:, None, :]
    rate = jnp.exp(-inv_y)
    rate_y = jnp.broadcast_to(rate.T[:, :, None], (scales, slabs, 128))
    smoothed, y_edges = x_pass(ctrl, gathered, carry, inv_rows, rate_y, tile, width, subs)
    arrived = lax.all_to_all(y_edges, "sub", split_axis=0, concat_axis=0, tiled=True)
    summed = y_carries(arrived, inv_y, rows, subs, me * each, each)
    returned = lax.all_to_all(summed, "sub", split_axis=0, concat_axis=0, tiled=True)
    carries = returned.reshape(subs, 2 * scales, each, width).transpose(1, 0, 2, 3)
    carries = carries.reshape(2 * scales, slabs, width)
    gain = (amplitude * (1.0 - rate) * (1.0 - rate)).T
    gain = jnp.broadcast_to(gain[:, :, None], (scales, slabs, 128))
    params = jnp.concatenate([rate_y, gain], axis=0)
    first = (me == 0).astype(jnp.int32)[None]
    increment, wind = y_pass(first, smoothed, carries, params, cols)
    return (increment.transpose(0, 2, 1), wind.transpose(0, 1, 3, 2))


def solution(mesh):
    placed = (P("sub", "col", None), P(), P(), P(), P())
    return jax.shard_map(
        per_device,
        mesh=mesh,
        in_specs=placed,
        out_specs=(P("sub", "col", None), P(None, "sub", "col", None)),
        check_vma=False,
    )
```

time: 484 us -> 152 us (0.31); the launches traced: 476 us -> 152 us
  blocking collectives: 111 us -> 0 us
  local copies, waits for them, and re-layouts: 96.8 us -> 4.33 us
  matrix products: 85.1 us -> 0 us
  Pallas kernels: 0 us -> 75.9 us
  other arithmetic: 66.3 us -> 8.05 us
  waiting for transfers between devices: 93 us -> 40.1 us
  starting transfers between devices: 14.7 us -> 9.18 us
  between operations: 9.15 us -> 14.4 us
    all_to_all x1 -> x0, blocking collectives: 111 us -> none  [send_back(): lax.all_to_all(arranged.reshape(sub_count * col_count * layers, band_rows...]
    dot_general x24 -> x0, matrix products: 85.1 us -> none  [the longest x12 82.8 us: local_solve(): jnp.einsum(spec('t', 'j') + ',sij->' + spec('t', 'i'), pieces, kernel, pr...]
    pallas_call x0 -> x3, Pallas kernels: none -> 75.9 us  [the longest x1 39.2 us: x_pass(): pl.pallas_call(functools.partial(x_kernel, tile, scales), grid=(slabs //...]
    all_to_all x1 -> x2, waiting for transfers between devices: 88.3 us -> 22.7 us  [the longest x1 11.6 us: per_device(): lax.all_to_all(y_edges, 'sub', split_axis=0, concat_axis=0, tiled=True)]
    all_to_all x2 -> x0, other arithmetic: 30.4 us -> none  [the longest x1 15.2 us: per_device(): lax.all_to_all(flat, ('sub', 'col'), split_axis=0, concat_axis=0, tiled=T...]
    another operation x4 -> x1, local copies, waits for them, and re-layouts: 27.5 us -> 0.69 us  [per_device(): inv_rows = jnp.repeat(inv_x, tile, axis=1)[:, None, :]]
    unnamed x22 -> x2, local copies, waits for them, and re-layouts: 23.8 us -> 0.01 us
    all_gather x0 -> x1, waiting for transfers between devices: none -> 17.4 us  [per_device(): gathered = lax.all_gather(edges, 'col')]
  transfers between devices with their start and end apart: 5 -> 3, of which waited for: 3 -> 3; matrix products, arithmetic and copies ran while one was open for 4% -> 4% of each run, Pallas kernels for 0% -> 0%
where the time goes in v1:
time: 152 us
  Pallas kernels  75.9 us (50%)
  waiting for transfers between devices  40.1 us (26%)
  between operations  14.4 us (9%)
  starting transfers between devices  9.18 us (6%)
  other arithmetic  8.05 us (5%)
  local copies, waits for them, and re-layouts  4.33 us (3%)
    pallas_call x1, Pallas kernels, x_pass(): pl.pallas_call(functools.partial(x_kernel, tile, scales), grid=(slabs //...  39.2 us
    pallas_call x1, Pallas kernels, y_pass(): pl.pallas_call(functools.partial(y_kernel, scales), grid=(slabs // block,...  27 us
    all_gather x1, waiting for transfers between devices, per_device(): gathered = lax.all_gather(edges, 'col')  17.4 us
    all_to_all x1, waiting for transfers between devices, per_device(): lax.all_to_all(y_edges, 'sub', split_axis=0, concat_axis=0, tiled=True)  11.6 us
    all_to_all x1, waiting for transfers between devices, per_device(): lax.all_to_all(summed, 'sub', split_axis=0, concat_axis=0, tiled=True)  11.1 us
    pallas_call x1, Pallas kernels, x_edges(): pl.pallas_call(functools.partial(edge_kernel, tile), grid=(slabs // group...  9.76 us
    all_to_all x1, starting transfers between devices, per_device(): lax.all_to_all(y_edges, 'sub', split_axis=0, concat_axis=0, tiled=True)  5.5 us
    all_to_all x1, starting transfers between devices, per_device(): lax.all_to_all(summed, 'sub', split_axis=0, concat_axis=0, tiled=True)  3.64 us
  transfers between devices with their start and end apart: 3, of which 3 were waited for; matrix products, arithmetic and copies ran while one was open for 4% of the time, Pallas kernels for 0%

profile of v1, /device:TPU:0, one launch (start us, length us, event | category | flops | bytes accessed | tf_op | source)
XLA Modules:
  0.0 152.0 jit_solution(3480015554267714635)
XLA Ops:
  7.2 0.0 all-gather.3.cloned.1.call-start
  7.2 0.7 fusion.9
  7.9 0.8 multiply_reduce_fusion
  8.7 0.1 copy.33
  8.8 0.1 copy.32
  8.9 0.1 pad.39.clone
  9.0 0.1 exponential_multiply_fusion.1
  9.1 0.7 maximum_maximum_fusion.weight_ref
  9.8 9.8 %x_edges.1 = f32[32,24,96]{2,1,0:T(8,128)} custom-call(f32[96,32,384]{2,1,0:T(8,128)} %bitcast.70, f32[32,8,128]{2,1,0:T(8,128)} %maximum_maximum_fusion.weight_ref), custom_call_target="tpu_custom_call" | custom-call | tf_op jit(solution)/shard_map/x_edges/pallas_call | solution.py:97
  19.6 0.0 all-gather.3.cloned.1.call-update
  19.8 0.1 dynamic-slice_bitcast_fusion
  19.9 0.1 mul.640
  20.0 0.1 compare_and_fusion.3
  20.1 0.1 copy.34
  20.2 0.1 compare_and_fusion.2
  20.2 0.1 copy.35
  20.4 0.1 copy.38
  20.5 0.1 convert_negate_fusion
  20.6 0.1 copy.37
  20.7 0.1 multiply_negate_fusion
  20.7 0.1 copy.39
  20.8 0.1 copy.40
  20.9 0.1 copy.41
  21.0 0.1 copy.36
  21.1 0.1 mul.607
  21.2 0.7 broadcast_in_dim_reshape.5.inv_ref
  21.9 0.1 convert_negate_fusion.1
  22.0 0.1 select_select_fusion.1
  22.1 2.7 %select_select_fusion.carry_ref = f32[32,96,32]{2,1,0:T(8,128)} fusion(f32[96,32]{1,0:T(8,128)S(1)} %copy.41, f32[32,32]{1,0:T(8,128)S(1)} %get-tuple-element.54, f32[32,32]{1,0:T(8,128)S(1)} %get-tuple-element.55, f32[96,32]{1,0:T(8,128)S(1)} %copy.40, f32[32,32]{1,0:T(8,128)S(1)} %get-tuple-element.56, f32[96,32]{1,0:T(8,128)S(1)} %copy.39, ...), kind=kLoop, calls=%fused_computation | loop fusion | flops 2260992 | bytes 480418 | tf_op jit(solution)/shard_map/jit(_where)/select_n | solution.py:75
  24.8 17.4 %all-gather.3.cloned.1.call-done = f32[128,24,96]{2,1,0:T(8,128)} async-done(((f32[32,24,96]{2,1,0:T(8,128)}), f32[128,24,96]{2,1,0:T(8,128)}) %all-gather.3.cloned.1.call-update) | async-done | bytes 1179664 | tf_op jit(solution)/shard_map/all_gather | solution.py:323
  42.1 0.7 broadcast_in_dim.257.ry_ref
  42.8 39.2 %x_pass.1 = (f32[3,96,32,512]{3,2,1,0:T(8,128)}, f32[8,24,512]{2,1,0:T(8,128)}) custom-call(f32[96,32,384]{2,1,0:T(8,128)} %bitcast.71, f32[4,32,24,96]{3,2,1,0:T(8,128)} %bitcast.73, f32[32,96,32]{2,1,0:T(8,128)} %select_select_fusion.carry_ref, f32[32,1,384]{2,1,0:T(1,128)} %broadcast_in_dim_reshape.5.inv_ref, f32[3,32,128]{2,1,0:T(8,128)} %broadcast_in_dim.257.ry_ref), custom_call_target="tpu_custom_call" | custom-call | tf_op jit(solution)/shard_map/x_pass/pallas_call | solution.py:189
  82.1 5.5 %all-to-all-start = ((f32[8,24,512]{2,1,0:T(8,128)}), f32[8,24,512]{2,1,0:T(8,128)S(1)}, u32[]{:S(2)}, u32[]{:S(2)}) async-start(f32[8,24,512]{2,1,0:T(8,128)} %get-tuple-element.7), calls=%async_computation | async-start | bytes 786432 | tf_op jit(solution)/shard_map/all_to_all | solution.py:329
  87.6 0.1 multiply_negate_fusion.2
  87.7 0.1 exponential_select_fusion
  87.8 0.1 pad_slice_fusion.21
  87.9 0.1 fusion.3
  88.1 11.6 %all-to-all-done = f32[8,24,512]{2,1,0:T(8,128)S(1)} async-done(((f32[8,24,512]{2,1,0:T(8,128)}), f32[8,24,512]{2,1,0:T(8,128)S(1)}, u32[]{:S(2)}, u32[]{:S(2)}) %all-to-all-start) | async-done | bytes 393248 | tf_op jit(solution)/shard_map/all_to_all | solution.py:329
  99.8 0.0 copy-start
  100.0 1.3 multiply_add_fusion
  101.3 3.6 %all-to-all-start.1 = ((f32[8,24,512]{2,1,0:T(8,128)}), f32[8,24,512]{2,1,0:T(8,128)S(1)}, u32[]{:S(2)}, u32[]{:S(2)}) async-start(f32[8,24,512]{2,1,0:T(8,128)} %multiply_add_fusion), calls=%async_computation.1 | async-start | bytes 786432 | tf_op jit(solution)/shard_map/all_to_all | solution.py:331
  104.9 0.1 broadcast_in_dim.264
  105.0 0.0 copy-done
  105.0 0.7 pad_maximum_fusion.par_ref
  105.7 11.1 %all-to-all-done.1 = f32[8,24,512]{2,1,0:T(8,128)S(1)} async-done(((f32[8,24,512]{2,1,0:T(8,128)}), f32[8,24,512]{2,1,0:T(8,128)S(1)}, u32[]{:S(2)}, u32[]{:S(2)}) %all-to-all-start.1) | async-done | bytes 393248 | tf_op jit(solution)/shard_map/all_to_all | solution.py:331
  116.8 0.2 copy.43
  117.0 0.3 copy.44
  117.3 0.9 reshape.1038.carry_ref
  118.2 27.0 %y_pass.1 = (f32[96,32,384]{2,1,0:T(8,128)}, bf16[2,96,32,384]{3,2,1,0:T(8,128)(2,1)}) custom-call(s32[1]{0:T(128)} %bitcast.first_ref, f32[3,96,32,512]{3,2,1,0:T(8,128)} %get-tuple-element.6.w_ref, f32[6,32,512]{2,1,0:T(8,128)} %reshape.1038.carry_ref, f32[6,32,128]{2,1,0:T(8,128)} %pad_maximum_fusion.par_ref), custom_call_target="tpu_custom_call" | custom-call | tf_op jit(solution)/shard_map/y_pass/pallas_call | solution.py:288
  (40 shorter events, 0.3 us)
Async XLA Ops:
  7.2 35.0 %all-gather.3.cloned.1.call-start = ((), (), s32[]{:S(2)}) async-start(), calls=%async_computation.2 | async-start | bytes 1966080 | tf_op jit(solution)/shard_map/all_gather | solution.py:323
  82.1 17.6 %all-to-all-start = ((f32[8,24,512]{2,1,0:T(8,128)}), f32[8,24,512]{2,1,0:T(8,128)S(1)}, u32[]{:S(2)}, u32[]{:S(2)}) async-start(f32[8,24,512]{2,1,0:T(8,128)} %get-tuple-element.7), calls=%async_computation | async-start | bytes 786432 | tf_op jit(solution)/shard_map/all_to_all | solution.py:329
  99.8 5.2 %copy-start = (f32[3,32,128]{2,1,0:T(8,128)S(1)}, f32[3,32,128]{2,1,0:T(8,128)}, u32[]{:S(2)}) copy-start(f32[3,32,128]{2,1,0:T(8,128)} %broadcast_in_dim.257.ry_ref) | copy-start | bytes 147460
  101.3 15.5 %all-to-all-start.1 = ((f32[8,24,512]{2,1,0:T(8,128)}), f32[8,24,512]{2,1,0:T(8,128)S(1)}, u32[]{:S(2)}, u32[]{:S(2)}) async-start(f32[8,24,512]{2,1,0:T(8,128)} %multiply_add_fusion), calls=%async_computation.1 | async-start | bytes 786432 | tf_op jit(solution)/shard_map/all_to_all | solution.py:331
Sparse Core Ops, SparseCore 0:
  19.7 22.3 all-gather.2

commit v2 on v1

--- a/solution.py
+++ b/solution.py
@@ -6,7 +6,6 @@
 from jax.experimental.pallas import tpu as pltpu
 from jax.sharding import PartitionSpec as P
 
-highest = lax.Precision.HIGHEST
 group = 8
 vmem_bytes = 56 * 1024 * 1024
 
@@ -80,15 +79,29 @@
     return high, (value - high.astype(jnp.float32)).astype(jnp.bfloat16)
 
 
+def split_weights(value):
+    high, low = split(value)
+    top = jnp.concatenate([high, low], axis=1)
+    return jnp.concatenate([top, jnp.concatenate([high, jnp.zeros_like(low)], axis=1)], axis=0)
+
+
+def stacked_tiles(ctrl_ref, s, tile):
+    cols = ctrl_ref.shape[2]
+    pieces = [ctrl_ref[:, s, t * tile : (t + 1) * tile] for t in range(cols // tile)]
+    return jnp.concatenate(split(jnp.concatenate(pieces, axis=0)), axis=1)
+
+
 def edge_kernel(tile, ctrl_ref, weight_ref, out_ref):
     rows, slabs, cols = ctrl_ref.shape
     for s in range(slabs):
+        out = jnp.dot(
+            stacked_tiles(ctrl_ref, s, tile),
+            split_weights(weight_ref[s]),
+            preferred_element_type=jnp.float32,
+        )
+        out = out[:, :8] + out[:, 8:16]
         for t in range(cols // tile):
-            piece = ctrl_ref[:, s, t * tile : (t + 1) * tile]
-            out_ref[s, t * 8 : (t + 1) * 8, :] = lax.dot_general(
-                weight_ref[s], piece, (((1,), (1,)), ((), ())),
-                precision=highest, preferred_element_type=jnp.float32,
-            )
+            out_ref[s, t * 8 : (t + 1) * 8, :] = out[t * rows : (t + 1) * rows].T
 
 
 def x_edges(ctrl, weights, tile):
@@ -99,7 +112,7 @@
         grid=(slabs // group,),
         in_specs=[
             pl.BlockSpec((rows, group, cols), lambda i: (0, i, 0)),
-            pl.BlockSpec((group, 8, tile), lambda i: (i, 0, 0)),
+            pl.BlockSpec((group, tile, 8), lambda i: (i, 0, 0)),
         ],
         out_specs=pl.BlockSpec((group, local * 8, rows), lambda i: (i, 0, 0)),
         out_shape=jax.ShapeDtypeStruct((slabs, local * 8, rows), jnp.float32),
@@ -124,18 +137,22 @@
     for s in range(slabs):
         inv = inv_ref[s]
         r = jnp.exp(-inv)
-        high_k, low_k = split(jnp.exp(-dist * inv) * ((1.0 - r) / (1.0 + r)))
+        weights = split_weights(jnp.exp(-dist * inv) * ((1.0 - r) / (1.0 + r)))
         from_left = jnp.exp(-(pos + 1.0) * inv) / (1.0 + r)
         from_right = jnp.exp(-(tile - pos) * inv) / (1.0 + r)
         gathered = jnp.concatenate([gath_ref[d, s] for d in range(gath_ref.shape[0])], axis=0)
         carry = lax.dot_general(
-            gathered, carry_ref[s], (((0,), (0,)), ((), ())),
-            precision=highest, preferred_element_type=jnp.float32,
+            jnp.concatenate(split(gathered), axis=0), split_weights(carry_ref[s]),
+            (((0,), (0,)), ((), ())), preferred_element_type=jnp.float32,
+        )
+        kinds = carry.shape[1] // 2
+        carry = carry[:, :kinds] + carry[:, kinds:]
+        whole = jnp.dot(
+            stacked_tiles(ctrl_ref, s, tile), weights, preferred_element_type=jnp.float32
         )
         for t in range(local):
-            high, low = split(ctrl_ref[:, s, t * tile : (t + 1) * tile])
-            dot = functools.partial(jnp.dot, preferred_element_type=jnp.float32)
-            out = dot(high, high_k) + (dot(high, low_k) + dot(low, high_k))
+            out = whole[t * rows : (t + 1) * rows]
+            out = out[:, :lanes] + out[:, lanes:]
             for m in range(scales):
                 part = slice(m * tile, (m + 1) * tile)
                 at = t * 8 + m
@@ -209,31 +226,103 @@
     )(ctrl, gathered, carry, inv_rows, rate_y)
 
 
-def y_carries(arrived, inv_y, rows, subs, first_slab, each):
-    scales = inv_y.shape[1]
-    width = arrived.shape[2]
-    inv = lax.dynamic_slice_in_dim(inv_y, first_slab, each, 0).T.reshape(scales * each)
-    src = jnp.arange(subs, dtype=jnp.int32)[None, :, None]
-    dst = jnp.arange(subs, dtype=jnp.int32)[:, None, None]
-    inv = inv[None, None, :]
+def greet(axis, size):
+    me = lax.axis_index(axis)
+    barrier = pltpu.get_barrier_semaphore()
+    for k in range(1, size):
+        pl.semaphore_signal(
+            barrier, inc=1, device_id={axis: lax.rem(me + k, size)},
+            device_id_type=pl.DeviceIdType.MESH,
+        )
+    pl.semaphore_wait(barrier, size - 1)
+
+
+def send_all(axis, size, source, target, send_sems, recv_sems):
+    me = lax.axis_index(axis)
+    copies = []
+    for k in range(1, size):
+        partner = lax.rem(me + k, size)
+        copies.append(
+            pltpu.make_async_remote_copy(
+                src_ref=source(partner), dst_ref=target.at[me],
+                send_sem=send_sems.at[k], recv_sem=recv_sems.at[k],
+                device_id={axis: partner}, device_id_type=pl.DeviceIdType.MESH,
+            )
+        )
+        copies[-1].start()
+    return copies
+
+
+def gather_kernel(axis, size, own_ref, all_ref, send_sems, recv_sems):
+    greet(axis, size)
+    copies = send_all(axis, size, lambda p: own_ref, all_ref, send_sems, recv_sems)
+    all_ref[lax.axis_index(axis)] = own_ref[...]
+    for copy in copies:
+        copy.wait()
+
+
+def gather(own, axis):
+    size = lax.axis_size(axis)
+    vmem = pl.BlockSpec(memory_space=pltpu.VMEM)
+    return pl.pallas_call(
+        functools.partial(gather_kernel, axis, size),
+        in_specs=[vmem],
+        out_specs=vmem,
+        out_shape=jax.ShapeDtypeStruct((size,) + own.shape, own.dtype),
+        scratch_shapes=[pltpu.SemaphoreType.DMA((size,)), pltpu.SemaphoreType.DMA((size,))],
+        compiler_params=pltpu.CompilerParams(
+            collective_id=0, has_side_effects=True, vmem_limit_bytes=vmem_bytes
+        ),
+        name="x_gather",
+    )(own)
+
+
+def y_exchange_kernel(axis, size, edge_ref, rate_ref, out_ref, arrived, summed, *sems):
+    me = lax.axis_index(axis)
+    greet(axis, size)
+    copies = send_all(axis, size, lambda p: edge_ref.at[p], arrived, sems[0], sems[1])
+    arrived[me] = edge_ref[me]
+    for copy in copies:
+        copy.wait()
+    half = edge_ref.shape[1] // 2
+    width = edge_ref.shape[2]
+    r, r_band, gain = [
+        jnp.concatenate([rate_ref[k]] * (width // 128), axis=1) for k in range(3)
+    ]
+    value = jnp.zeros((half, width), jnp.float32)
+    for a in range(size):
+        summed[a, :half, :] = value
+        value = r_band * value + arrived[a, :half, :]
+    back = -r * value
+    summed[size - 1, half:, :] = jnp.zeros((half, width), jnp.float32)
+    for a in range(size - 1, 0, -1):
+        back = r_band * back + arrived[a, half:, :]
+        summed[a - 1, half:, :] = (r * summed[a, :half, :] + back) * gain
+    copies = send_all(axis, size, lambda p: summed.at[p], out_ref, sems[2], sems[3])
+    out_ref[me] = summed[me]
+    for copy in copies:
+        copy.wait()
+
+
+def y_exchange(y_edges, inv, rows, axis):
+    size = lax.axis_size(axis)
     r = jnp.exp(-inv)
-    r_tile = jnp.exp(-inv * rows)
-    parts = []
-    for is_fwd in (True, False):
-        flag = jnp.full((1, 1, 1), is_fwd)
-        c = fwd_weight(flag, src, dst, rows, inv)
-        d = bwd_weight(flag, src, dst, rows, subs, inv)
-        own = jnp.where((src == dst) & flag, 1.0, 0.0)
-        right = (r * (own + r_tile * c) + d) / ((1.0 + r) * (1.0 - r))
-        right = jnp.where(dst == subs - 1, 0.0, right)
-        parts.append(jnp.concatenate([c, right], axis=2))
-    half = scales * each
-    total = 0.0
-    for a in range(subs):
-        fwd = jnp.concatenate([arrived[a, :half]] * 2, axis=0)
-        bwd = jnp.concatenate([arrived[a, half:]] * 2, axis=0)
-        total = total + parts[0][:, a, :, None] * fwd[None] + parts[1][:, a, :, None] * bwd[None]
-    return total
+    rates = jnp.stack([r, jnp.exp(-inv * rows), 1.0 / ((1.0 + r) * (1.0 - r))])
+    rates = jnp.broadcast_to(rates[:, :, None], rates.shape + (128,))
+    vmem = pl.BlockSpec(memory_space=pltpu.VMEM)
+    shape = y_edges.shape
+    return pl.pallas_call(
+        functools.partial(y_exchange_kernel, axis, size),
+        in_specs=[vmem] * 2,
+        out_specs=vmem,
+        out_shape=jax.ShapeDtypeStruct(shape, jnp.float32),
+        scratch_shapes=[pltpu.VMEM(shape, jnp.float32)] * 2
+        + [pltpu.SemaphoreType.DMA((size,))] * 4,
+        compiler_params=pltpu.CompilerParams(
+            collective_id=1, has_side_effects=True, vmem_limit_bytes=vmem_bytes
+        ),
+        name="y_exchange",
+    )(y_edges, rates)
 
 
 def y_kernel(scales, first_ref, w_ref, carry_ref, par_ref, inc_ref, wind_ref, held):
@@ -253,33 +342,34 @@
             held[m, y] = state[m]
         return state
 
-    lax.fori_loop(0, rows, ahead, start, unroll=2)
+    lax.fori_loop(0, rows, ahead, start, unroll=4)
     ends = tuple(carry_ref[scales + m] for m in range(scales))
 
     def mix(state):
         return sum(widen(gains[m]) * state[m] for m in range(scales))
 
-    def back(i, carried):
+    def back(i, state):
         y = rows - 1 - i
-        state, after, later = carried
         state = tuple(widen(rates[m]) * state[m] + held[m, y] for m in range(scales))
         total = mix(state)
         here = total[:, :cols]
         inc_ref[y] = here
         east = pltpu.roll(total, width - 1, 1)[:, :cols] - pltpu.roll(total, 1, 1)[:, :cols]
         wind_ref[1, y] = (2.0 * east).astype(jnp.bfloat16)
-
-        @pl.when(i > 0)
-        def _():
-            wind_ref[0, y + 1] = (-2.0 * (later - here)).astype(jnp.bfloat16)
-
-        return state, here, after
-
+        return state
+
+    state = lax.fori_loop(0, rows, back, ends, unroll=4)
     below = mix(ends)[:, :cols]
-    state, after, later = lax.fori_loop(0, rows, back, (ends, below, below), unroll=2)
     above = mix(tuple(widen(rates[m]) * state[m] + start[m] for m in range(scales)))[:, :cols]
     above = jnp.where(first_ref[0] == 1, 0.0, above)
-    wind_ref[0, 0] = (-2.0 * (later - above)).astype(jnp.bfloat16)
+    wind_ref[0, 0] = (-2.0 * (inc_ref[1] - above)).astype(jnp.bfloat16)
+    wind_ref[0, rows - 1] = (-2.0 * (below - inc_ref[rows - 2])).astype(jnp.bfloat16)
+
+    def north(y, _):
+        wind_ref[0, y] = (-2.0 * (inc_ref[y + 1] - inc_ref[y - 1])).astype(jnp.bfloat16)
+        return _
+
+    lax.fori_loop(1, rows - 1, north, 0, unroll=2)
 
 
 def y_pass(first, smoothed, carries, params, cols):
@@ -319,16 +409,15 @@
     each = slabs // subs
     me = lax.axis_index("sub")
     ctrl = control.transpose(0, 2, 1)
-    edges = x_edges(ctrl, edge_weights(inv_x, tile), tile)
-    gathered = lax.all_gather(edges, "col")
+    edges = x_edges(ctrl, edge_weights(inv_x, tile).transpose(0, 2, 1), tile)
+    gathered = gather(edges, "col")
     carry = carry_matrix(inv_x, tile, local, cols_n, lax.axis_index("col"))
     inv_rows = jnp.repeat(inv_x, tile, axis=1)[:, None, :]
     rate = jnp.exp(-inv_y)
     rate_y = jnp.broadcast_to(rate.T[:, :, None], (scales, slabs, 128))
     smoothed, y_edges = x_pass(ctrl, gathered, carry, inv_rows, rate_y, tile, width, subs)
-    arrived = lax.all_to_all(y_edges, "sub", split_axis=0, concat_axis=0, tiled=True)
-    summed = y_carries(arrived, inv_y, rows, subs, me * each, each)
-    returned = lax.all_to_all(summed, "sub", split_axis=0, concat_axis=0, tiled=True)
+    owned = lax.dynamic_slice_in_dim(inv_y, me * each, each, 0).T.reshape(scales * each)
+    returned = y_exchange(y_edges, owned, rows, "sub")
     carries = returned.reshape(subs, 2 * scales, each, width).transpose(1, 0, 2, 3)
     carries = carries.reshape(2 * scales, slabs, width)
     gain = (amplitude * (1.0 - rate) * (1.0 - rate)).T

time: 152 us -> 127 us (0.84); the launches traced: 152 us -> 125 us
  waiting for transfers between devices: 40.1 us -> 0 us
  Pallas kernels: 75.9 us -> 112 us
  between operations: 14.4 us -> 0.84 us
  starting transfers between devices: 9.18 us -> 0 us
  other arithmetic: 8.05 us -> 5.61 us
  local copies, waits for them, and re-layouts: 4.33 us -> 6.75 us
    pallas_call x0 -> x2, Pallas kernels: none -> 45.9 us  [the longest x1 23.3 us: y_exchange(): pl.pallas_call(functools.partial(y_exchange_kernel, axis, size), in_specs...]
    all_to_all x2 -> x0, waiting for transfers between devices: 22.7 us -> none  [the longest x1 11.6 us: per_device(): lax.all_to_all(y_edges, 'sub', split_axis=0, concat_axis=0, tiled=True)]
    all_gather x1 -> x0, waiting for transfers between devices: 17.4 us -> none  [per_device(): gathered = lax.all_gather(edges, 'col')]
    pallas_call x1, Pallas kernels: 27 us -> 15.6 us  [y_pass(): pl.pallas_call(functools.partial(y_kernel, scales), grid=(slabs // block,...]
    all_to_all x2 -> x0, starting transfers between devices: 9.14 us -> none  [the longest x1 5.5 us: per_device(): lax.all_to_all(y_edges, 'sub', split_axis=0, concat_axis=0, tiled=True)]
    pallas_call x1, Pallas kernels: 39.2 us -> 43.4 us  [x_pass(): pl.pallas_call(functools.partial(x_kernel, tile, scales), grid=(slabs //...]
    pallas_call x1, Pallas kernels: 9.76 us -> 6.99 us  [x_edges(): pl.pallas_call(functools.partial(edge_kernel, tile), grid=(slabs // group...]
    concatenate x1 -> x2, local copies, waits for them, and re-layouts: 0.08 us -> 2 us  [edge_weights(): return jnp.concatenate([fwd, bwd, pad], axis=1)]
  transfers between devices with their start and end apart: 3 -> 0, of which waited for: 3 -> 0; matrix products, arithmetic and copies ran while one was open for 4% -> 0% of each run, Pallas kernels for 0% -> 0%
where the time goes in v2:
time: 127 us; the launch traced here: 125 us
  Pallas kernels  112 us (88%)
  local copies, waits for them, and re-layouts  6.75 us (5%)
  other arithmetic  5.61 us (4%)
    pallas_call x1, Pallas kernels, x_pass(): pl.pallas_call(functools.partial(x_kernel, tile, scales), grid=(slabs //...  43.4 us
    pallas_call x1, Pallas kernels, y_exchange(): pl.pallas_call(functools.partial(y_exchange_kernel, axis, size), in_specs...  23.3 us
    pallas_call x1, Pallas kernels, gather(): pl.pallas_call(functools.partial(gather_kernel, axis, size), in_specs=[vm...  22.6 us
    pallas_call x1, Pallas kernels, y_pass(): pl.pallas_call(functools.partial(y_kernel, scales), grid=(slabs // block,...  15.6 us
    pallas_call x1, Pallas kernels, x_edges(): pl.pallas_call(functools.partial(edge_kernel, tile), grid=(slabs // group...  6.99 us
    select_n x1, other arithmetic, carry_matrix(): return jnp.where(valid, value, 0.0)  2.66 us

profile of v2, /device:TPU:0, one launch (start us, length us, event | category | flops | bytes accessed | tf_op | source)
XLA Modules:
  0.0 125.1 jit_solution(13556096657674333664)
XLA Ops:
  0.7 0.1 pad.7.clone
  0.9 0.1 compare_and_fusion.3
  0.9 0.7 fusion.2
  1.6 0.8 multiply_reduce_fusion
  2.5 0.1 exponential_bitcast_fusion
  2.5 0.1 exp.101
  2.6 0.1 exp.98
  2.7 0.1 copy.38
  2.9 0.1 compare_and_fusion.2
  2.9 0.1 copy.39
  3.0 0.1 copy.42
  3.2 0.1 copy.36
  3.3 0.1 copy.35
  3.3 0.1 convert_negate_fusion
  3.4 0.7 broadcast_in_dim.185.rate_ref
  4.1 0.1 copy.41
  4.2 0.1 broadcast_in_dim.186
  4.3 0.1 broadcast_in_dim.184.ry_ref
  4.3 0.0 copy-start
  4.3 0.7 pad_maximum_fusion.par_ref
  5.0 0.1 select_select_fusion.1
  5.1 0.1 multiply_negate_fusion
  5.2 0.1 copy.43
  5.3 0.1 copy.44
  5.4 0.1 copy.45
  5.5 0.1 copy.40
  5.5 0.1 mul.247
  5.6 0.7 broadcast_in_dim_reshape.4.inv_ref
  6.3 0.1 exponential_multiply_fusion.1
  6.5 0.1 maximum_maximum_fusion
  6.6 2.7 %select_select_fusion.carry_ref = f32[32,96,32]{2,1,0:T(8,128)} fusion(f32[96,32]{1,0:T(8,128)S(1)} %copy.45, f32[32,32]{1,0:T(8,128)S(1)} %get-tuple-element.20, f32[32,32]{1,0:T(8,128)S(1)} %get-tuple-element.21, f32[96,32]{1,0:T(8,128)S(1)} %copy.44, f32[32,32]{1,0:T(8,128)S(1)} %get-tuple-element.22, f32[96,32]{1,0:T(8,128)S(1)} %copy.43, ...), kind=kLoop, calls=%fused_computation | loop fusion | flops 2260992 | bytes 480418 | tf_op jit(solution)/shard_map/jit(_where)/select_n | solution.py:74
  9.2 0.0 copy-done
  9.2 1.9 %copy.37 = f32[32,8,128]{1,2,0:T(8,128)} copy(f32[32,8,128]{2,1,0:T(8,128)S(1)} %maximum_maximum_fusion) | data formatting | bytes 262144 | tf_op jit(solution)/shard_map/concatenate | solution.py:43
  11.2 7.0 %x_edges.1.own_ref = f32[32,24,96]{2,1,0:T(8,128)} custom-call(f32[96,32,384]{2,1,0:T(8,128)} %bitcast.24, f32[32,128,8]{2,1,0:T(8,128)} %bitcast.26), custom_call_target="tpu_custom_call" | custom-call | tf_op jit(solution)/shard_map/x_edges/pallas_call | solution.py:110
  18.1 22.6 %x_gather.1.gath_ref = f32[4,32,24,96]{3,2,1,0:T(8,128)} custom-call(f32[32,24,96]{2,1,0:T(8,128)} %x_edges.1.own_ref), custom_call_target="tpu_custom_call" | custom-call | tf_op jit(solution)/shard_map/x_gather/pallas_call | solution.py:267
  40.7 43.4 %x_pass.1 = (f32[3,96,32,512]{3,2,1,0:T(8,128)}, f32[8,24,512]{2,1,0:T(8,128)}) custom-call(f32[96,32,384]{2,1,0:T(8,128)} %bitcast.25, f32[4,32,24,96]{3,2,1,0:T(8,128)} %x_gather.1.gath_ref, f32[32,96,32]{2,1,0:T(8,128)} %select_select_fusion.carry_ref, f32[32,1,384]{2,1,0:T(1,128)} %broadcast_in_dim_reshape.4.inv_ref, f32[3,32,128]{2,1,0:T(8,128)} %copy-done), custom_call_target="tpu_custom_call" | custom-call | tf_op jit(solution)/shard_map/x_pass/pallas_call | solution.py:206
  84.1 23.3 %y_exchange.1 = f32[8,24,512]{2,1,0:T(8,128)} custom-call(f32[8,24,512]{2,1,0:T(8,128)} %get-tuple-element.7.edge_ref, f32[3,12,128]{2,1,0:T(8,128)} %broadcast_in_dim.185.rate_ref), custom_call_target="tpu_custom_call" | custom-call | tf_op jit(solution)/shard_map/y_exchange/pallas_call | solution.py:314
  107.4 1.1 reshape.864
  108.6 0.9 reshape.865.carry_ref
  109.5 15.6 %y_pass.1 = (f32[96,32,384]{2,1,0:T(8,128)}, bf16[2,96,32,384]{3,2,1,0:T(8,128)(2,1)}) custom-call(s32[1]{0:T(128)} %bitcast.first_ref, f32[3,96,32,512]{3,2,1,0:T(8,128)} %get-tuple-element.6.w_ref, f32[6,32,512]{2,1,0:T(8,128)} %reshape.865.carry_ref, f32[6,32,128]{2,1,0:T(8,128)} %pad_maximum_fusion.par_ref), custom_call_target="tpu_custom_call" | custom-call | tf_op jit(solution)/shard_map/y_pass/pallas_call | solution.py:378
  (19 shorter events, 0.2 us)
Async XLA Ops:
  4.3 4.9 %copy-start = (f32[3,32,128]{2,1,0:T(8,128)}, f32[3,32,128]{2,1,0:T(8,128)S(1)}, u32[]{:S(2)}) copy-start(f32[3,32,128]{2,1,0:T(8,128)S(1)} %broadcast_in_dim.184.ry_ref) | copy-start | bytes 147460

commit v3 on v2

--- a/solution.py
+++ b/solution.py
@@ -121,7 +121,7 @@
     )(ctrl, weights)
 
 
-def x_kernel(tile, scales, ctrl_ref, gath_ref, carry_ref, inv_ref, ry_ref, w_ref, ye_ref):
+def x_kernel(tile, scales, ctrl_ref, gath_ref, carry_ref, inv_ref, ry_ref, w_ref, ye_ref, held):
     rows, slabs, cols = ctrl_ref.shape
     local = cols // tile
     width = w_ref.shape[3]
@@ -134,6 +134,13 @@
     one_scale = sum((one >= m * tile).astype(jnp.int32) for m in range(1, scales))
     pos = (one - one_scale * tile).astype(jnp.float32)
     spot = lax.broadcasted_iota(jnp.int32, (rows, width - cols), 1)
+
+    def put(m, s, start, stop, value):
+        if tile != 128:
+            w_ref[m, :, s, start:stop] = value
+            return
+        held[m, s, :, start:stop] = value
+
     for s in range(slabs):
         inv = inv_ref[s]
         r = jnp.exp(-inv)
@@ -156,18 +163,22 @@
             for m in range(scales):
                 part = slice(m * tile, (m + 1) * tile)
                 at = t * 8 + m
-                w_ref[m, :, s, t * tile : (t + 1) * tile] = (
+                put(m, s, t * tile, (t + 1) * tile, (
                     out[:, part]
                     + carry[:, at : at + 1] * from_left[:, part]
                     + carry[:, at + scales : at + scales + 1] * from_right[:, part]
-                )
+                ))
         for m in range(scales):
             at = local * 8 + m
             left = carry[:, at : at + 1]
             right = carry[:, at + scales : at + scales + 1]
-            w_ref[m, :, s, cols:] = jnp.where(
-                spot == 0, right, jnp.where(spot == width - cols - 1, left, 0.0)
-            )
+            halo = jnp.where(spot == 0, right, jnp.where(spot == width - cols - 1, left, 0.0))
+            put(m, s, cols, width, halo)
+
+    if tile == 128:
+        for m in range(scales):
+            for at in range(0, width, 128):
+                w_ref[m, :, :, at : at + 128] = jnp.swapaxes(held[m, :, :, at : at + 128], 0, 1)
 
     owners = ye_ref.shape[0]
     each = slabs // owners
@@ -221,6 +232,7 @@
             jax.ShapeDtypeStruct((scales, rows, slabs, width), jnp.float32),
             jax.ShapeDtypeStruct((subs, 2 * scales * each, width), jnp.float32),
         ],
+        scratch_shapes=[pltpu.VMEM((scales, group, rows, width), jnp.float32)],
         compiler_params=pltpu.CompilerParams(vmem_limit_bytes=vmem_bytes),
         name="x_pass",
     )(ctrl, gathered, carry, inv_rows, rate_y)

time: 127 us -> 119 us (0.937)
  Pallas kernels: 112 us -> 104 us
    pallas_call x1, Pallas kernels: 43.4 us -> 35.3 us  [x_pass(): pl.pallas_call(functools.partial(x_kernel, tile, scales), grid=(slabs //...]
where the time goes in v3:
time: 119 us; the launch traced here: 117 us
  Pallas kernels  104 us (87%)
  local copies, waits for them, and re-layouts  6.75 us (6%)
  other arithmetic  5.61 us (5%)
    pallas_call x1, Pallas kernels, x_pass(): pl.pallas_call(functools.partial(x_kernel, tile, scales), grid=(slabs //...  35.3 us
    pallas_call x1, Pallas kernels, y_exchange(): pl.pallas_call(functools.partial(y_exchange_kernel, axis, size), in_specs...  23.3 us
    pallas_call x1, Pallas kernels, gather(): pl.pallas_call(functools.partial(gather_kernel, axis, size), in_specs=[vm...  22.6 us
    pallas_call x1, Pallas kernels, y_pass(): pl.pallas_call(functools.partial(y_kernel, scales), grid=(slabs // block,...  15.6 us
    pallas_call x1, Pallas kernels, x_edges(): pl.pallas_call(functools.partial(edge_kernel, tile), grid=(slabs // group...  6.99 us
    select_n x1, other arithmetic, carry_matrix(): return jnp.where(valid, value, 0.0)  2.66 us

profile of v3, /device:TPU:0, one launch (start us, length us, event | category | flops | bytes accessed | tf_op | source)
XLA Modules:
  0.0 117.0 jit_solution(5733922860463257078)
XLA Ops:
  0.7 0.1 pad.7.clone
  0.9 0.1 compare_and_fusion.3
  0.9 0.7 fusion.2
  1.6 0.8 multiply_reduce_fusion
  2.5 0.1 exponential_bitcast_fusion
  2.5 0.1 exp.101
  2.6 0.1 exp.98
  2.7 0.1 copy.38
  2.9 0.1 compare_and_fusion.2
  2.9 0.1 copy.39
  3.0 0.1 copy.42
  3.2 0.1 copy.36
  3.3 0.1 copy.35
  3.3 0.1 convert_negate_fusion
  3.4 0.7 broadcast_in_dim.185.rate_ref
  4.1 0.1 copy.41
  4.2 0.1 broadcast_in_dim.186
  4.3 0.1 broadcast_in_dim.184.ry_ref
  4.3 0.0 copy-start
  4.3 0.7 pad_maximum_fusion.par_ref
  5.0 0.1 select_select_fusion.1
  5.1 0.1 multiply_negate_fusion
  5.2 0.1 copy.43
  5.3 0.1 copy.44
  5.4 0.1 copy.45
  5.5 0.1 copy.40
  5.5 0.1 mul.247
  5.6 0.7 broadcast_in_dim_reshape.4.inv_ref
  6.3 0.1 exponential_multiply_fusion.1
  6.5 0.1 maximum_maximum_fusion
  6.6 2.7 %select_select_fusion.carry_ref = f32[32,96,32]{2,1,0:T(8,128)} fusion(f32[96,32]{1,0:T(8,128)S(1)} %copy.45, f32[32,32]{1,0:T(8,128)S(1)} %get-tuple-element.20, f32[32,32]{1,0:T(8,128)S(1)} %get-tuple-element.21, f32[96,32]{1,0:T(8,128)S(1)} %copy.44, f32[32,32]{1,0:T(8,128)S(1)} %get-tuple-element.22, f32[96,32]{1,0:T(8,128)S(1)} %copy.43, ...), kind=kLoop, calls=%fused_computation | loop fusion | flops 2260992 | bytes 480418 | tf_op jit(solution)/shard_map/jit(_where)/select_n | solution.py:74
  9.2 0.0 copy-done
  9.2 1.9 %copy.37 = f32[32,8,128]{1,2,0:T(8,128)} copy(f32[32,8,128]{2,1,0:T(8,128)S(1)} %maximum_maximum_fusion) | data formatting | bytes 262144 | tf_op jit(solution)/shard_map/concatenate | solution.py:43
  11.2 7.0 %x_edges.1.own_ref = f32[32,24,96]{2,1,0:T(8,128)} custom-call(f32[96,32,384]{2,1,0:T(8,128)} %bitcast.24, f32[32,128,8]{2,1,0:T(8,128)} %bitcast.26), custom_call_target="tpu_custom_call" | custom-call | tf_op jit(solution)/shard_map/x_edges/pallas_call | solution.py:110
  18.1 22.6 %x_gather.1.gath_ref = f32[4,32,24,96]{3,2,1,0:T(8,128)} custom-call(f32[32,24,96]{2,1,0:T(8,128)} %x_edges.1.own_ref), custom_call_target="tpu_custom_call" | custom-call | tf_op jit(solution)/shard_map/x_gather/pallas_call | solution.py:279
  40.7 35.3 %x_pass.1 = (f32[3,96,32,512]{3,2,1,0:T(8,128)}, f32[8,24,512]{2,1,0:T(8,128)}) custom-call(f32[96,32,384]{2,1,0:T(8,128)} %bitcast.25, f32[4,32,24,96]{3,2,1,0:T(8,128)} %x_gather.1.gath_ref, f32[32,96,32]{2,1,0:T(8,128)} %select_select_fusion.carry_ref, f32[32,1,384]{2,1,0:T(1,128)} %broadcast_in_dim_reshape.4.inv_ref, f32[3,32,128]{2,1,0:T(8,128)} %copy-done), custom_call_target="tpu_custom_call" | custom-call | tf_op jit(solution)/shard_map/x_pass/pallas_call | solution.py:217
  76.1 23.3 %y_exchange.1 = f32[8,24,512]{2,1,0:T(8,128)} custom-call(f32[8,24,512]{2,1,0:T(8,128)} %get-tuple-element.7.edge_ref, f32[3,12,128]{2,1,0:T(8,128)} %broadcast_in_dim.185.rate_ref), custom_call_target="tpu_custom_call" | custom-call | tf_op jit(solution)/shard_map/y_exchange/pallas_call | solution.py:326
  99.4 1.1 reshape.864
  100.5 0.9 reshape.865.carry_ref
  101.4 15.6 %y_pass.1 = (f32[96,32,384]{2,1,0:T(8,128)}, bf16[2,96,32,384]{3,2,1,0:T(8,128)(2,1)}) custom-call(s32[1]{0:T(128)} %bitcast.first_ref, f32[3,96,32,512]{3,2,1,0:T(8,128)} %get-tuple-element.6.w_ref, f32[6,32,512]{2,1,0:T(8,128)} %reshape.865.carry_ref, f32[6,32,128]{2,1,0:T(8,128)} %pad_maximum_fusion.par_ref), custom_call_target="tpu_custom_call" | custom-call | tf_op jit(solution)/shard_map/y_pass/pallas_call | solution.py:390
  (19 shorter events, 0.2 us)
Async XLA Ops:
  4.3 4.9 %copy-start = (f32[3,32,128]{2,1,0:T(8,128)}, f32[3,32,128]{2,1,0:T(8,128)S(1)}, u32[]{:S(2)}) copy-start(f32[3,32,128]{2,1,0:T(8,128)S(1)} %broadcast_in_dim.184.ry_ref) | copy-start | bytes 147460
